TPU v7x, 512 devices: a whole 4x8x8 slice. The times are simulated.
512 devices in a mesh: ctx: 32 (over y, z_lo, core), tp: 4 (over z_hi), dp: 4 (over x).
Axes of the slice: x: 4, y: 8, z: 8 (z_hi: 4, z_lo: 2; z = z_hi * 2 + z_lo), core: 2. Of those that a mesh axis runs over, the one named last changes fastest.
Arguments:
- queries: bfloat16 [16384, 8192], P(('dp', 'ctx'), 'tp'), parts along dimension 0
- keys: bfloat16 [16384, 1024], P(('dp', 'ctx'), 'tp'), parts along dimension 0
- values: bfloat16 [16384, 1024], P(('dp', 'ctx'), 'tp'), parts along dimension 0, may hold values from -6 to 6
- loader_pos: int32 [16384], P(('dp', 'ctx')), parts along dimension 0, may hold values from 0 to 4095, as said below
- reset_pos: int32 [16384], P(('dp', 'ctx')), parts along dimension 0, may hold values from 0 to 2047, as said below
- doc_starts: int32 [64], P('dp'), parts along dimension 0, may hold values from 0 to 4095, as said below
Outputs:
- attention: bfloat16 [16384, 8192], P(('dp', 'ctx'), 'tp'), parts along dimension 0
There are 4 independent parts, one for each index of `dp`. A program takes and returns all parts, laid end to end along the dimension named above; each array names one. Nothing has to cross between parts.
Inputs may be any that keep to these rules, and one draw needn't show every extreme that they name: `loader_pos`: a permutation of the 4096 positions; split the positions into 64 blocks of 64 and let shard i own blocks i and 63 - i: the rows of each device of ctx hold exactly 4 positions owned by each shard. `reset_pos`: the position of each loader row's token within its document, loader_pos minus the start of its document. `doc_starts`: increasing, the first 0; every document has 1 to 2048 tokens and one has exactly 2048.
All inputs are finite; a program needn't handle non-finite values.
Results may differ from a plain program's by a relative error of at most 0.006.
Values may be sent and summed in bfloat16 or wider, within the bound.
A program may use at most 64 MiB of HBM per device.

v0:
```python
import math

import jax
import jax.numpy as jnp
from jax import lax
from jax.sharding import PartitionSpec as P

HEAD_WIDTH = 128


ROPE_BASE = 1000000.0


def rotate(row_block, positions):
    row_count = row_block.shape[0]
    q_heads = row_block.shape[1] // HEAD_WIDTH
    lanes = row_block.astype(jnp.float32).reshape(row_count, q_heads, HEAD_WIDTH)
    frequency = ROPE_BASE ** (-jnp.arange(HEAD_WIDTH // 2, dtype=jnp.float32) * 2.0 / HEAD_WIDTH)
    angles = positions.astype(jnp.float32)[:, None] * frequency[None, :]
    cosine = jnp.cos(angles)[:, None, :]
    sine_term = jnp.sin(angles)[:, None, :]
    lower_half = lanes[..., : HEAD_WIDTH // 2]
    upper_half = lanes[..., HEAD_WIDTH // 2 :]
    result = jnp.concatenate(
        [
            lower_half * cosine - upper_half * sine_term,
            upper_half * cosine + lower_half * sine_term,
        ],
        axis=-1,
    )
    return result.reshape(row_count, q_heads * HEAD_WIDTH).astype(jnp.bfloat16)


def document_of(positions, doc_starts):
    return (
        jnp.sum(
            (doc_starts[None, :] <= positions[:, None]).astype(jnp.int32), axis=1, dtype=jnp.int32
        )
        - 1
    )


def attend(state_now, query_grouped, q_pos, q_doc, key_piece, value_piece, key_pos, doc_starts):
    piece_rows = key_piece.shape[0]
    kv_heads = query_grouped.shape[1]
    sub_rows = math.gcd(piece_rows, 512)
    step_count = piece_rows // sub_rows
    score_scale = 1.0 / math.sqrt(HEAD_WIDTH)
    key_blocks = key_piece.reshape(step_count, sub_rows, kv_heads, HEAD_WIDTH)
    value_blocks = value_piece.reshape(step_count, sub_rows, kv_heads, HEAD_WIDTH)
    pos_blocks = key_pos.reshape(step_count, sub_rows)

    def one_step(state_in, block_args):
        key_block, value_block, pos_block = block_args
        key_doc = document_of(pos_block, doc_starts)
        allowed = (q_doc[:, None] == key_doc[None, :]) & (pos_block[None, :] <= q_pos[:, None])
        maxima, totals, accumulated = state_in
        scores = (
            jnp.einsum(
                "tgjd,kgd->gjtk", query_grouped, key_block, preferred_element_type=jnp.float32
            )
            * score_scale
        )
        scores = jnp.where(allowed, scores, -1e30)
        updated = jnp.maximum(maxima, jnp.max(scores, axis=-1))
        rescale = jnp.exp(maxima - updated)
        weights = jnp.where(allowed, jnp.exp(scores - updated[..., None]), 0.0).astype(jnp.bfloat16)
        totals = totals * rescale + jnp.sum(weights, axis=-1, dtype=jnp.float32)
        accumulated = accumulated * rescale[..., None] + jnp.einsum(
            "gjtk,kgd->gjtd", weights, value_block, preferred_element_type=jnp.float32
        )
        state_out = (updated, totals, accumulated)
        return (state_out, None)

    state_now, _ = lax.scan(one_step, state_now, (key_blocks, value_blocks, pos_blocks))
    return state_now


def finish(state_now, row_count):
    maxima, totals, accumulated = state_now
    result = accumulated / totals[..., None]
    kv_heads, heads_per_group = (result.shape[0], result.shape[1])
    return (
        jnp.transpose(result, (2, 0, 1, 3))
        .reshape(row_count, kv_heads * heads_per_group * HEAD_WIDTH)
        .astype(jnp.bfloat16)
    )


def on_device(queries, keys, values, loader_pos, reset_pos, doc_starts):
    row_count = queries.shape[0]
    q_heads = queries.shape[1] // HEAD_WIDTH
    kv_heads = keys.shape[1] // HEAD_WIDTH
    heads_per_group = q_heads // kv_heads
    ctx_count = lax.axis_size("ctx")
    my_index = lax.axis_index("ctx")
    half_rows = row_count // 2
    q_rot = rotate(queries, reset_pos)
    k_rot = rotate(keys, reset_pos)
    initial = (
        jnp.full((kv_heads, heads_per_group, row_count), -1e30, jnp.float32),
        jnp.zeros((kv_heads, heads_per_group, row_count), jnp.float32),
        jnp.zeros((kv_heads, heads_per_group, row_count, HEAD_WIDTH), jnp.float32),
    )

    def owned_position(shard_ids, offsets):
        block_of = jnp.where(offsets < half_rows, shard_ids, 2 * ctx_count - 1 - shard_ids)
        return block_of * half_rows + offsets % half_rows

    block_num = loader_pos // half_rows
    owner_shard = jnp.where(block_num < ctx_count, block_num, 2 * ctx_count - 1 - block_num)
    send_order = jnp.argsort(owner_shard * (row_count * ctx_count) + loader_pos)
    outgoing = (q_rot[send_order], k_rot[send_order], values[send_order], loader_pos[send_order])
    got_q, got_k, got_v, got_pos = (
        lax.all_to_all(outgoing[0], "ctx", split_axis=0, concat_axis=0, tiled=True),
        lax.all_to_all(outgoing[1], "ctx", split_axis=0, concat_axis=0, tiled=True),
        lax.all_to_all(outgoing[2], "ctx", split_axis=0, concat_axis=0, tiled=True),
        lax.all_to_all(outgoing[3], "ctx", split_axis=0, concat_axis=0, tiled=True),
    )
    local_order = jnp.argsort(got_pos)
    q_local = got_q[local_order]
    k_local = got_k[local_order]
    v_local = got_v[local_order]
    q_pos = owned_position(my_index, jnp.arange(row_count, dtype=jnp.int32))
    q_doc = document_of(q_pos, doc_starts)
    query_grouped = q_local.reshape(row_count, kv_heads, heads_per_group, HEAD_WIDTH)
    key_piece = (
        lax.all_gather(k_local, "ctx", axis=0, tiled=True),
        lax.all_gather(v_local, "ctx", axis=0, tiled=True),
    )
    row_index = jnp.arange(key_piece[0].shape[0], dtype=jnp.int32)
    key_pos = owned_position(row_index // row_count, row_index % row_count)
    state_end = attend(
        initial, query_grouped, q_pos, q_doc, key_piece[0], key_piece[1], key_pos, doc_starts
    )
    out_local = finish(state_end, row_count)
    back_rows = out_local[jnp.argsort(local_order)]
    returned = lax.all_to_all(back_rows, "ctx", split_axis=0, concat_axis=0, tiled=True)
    return returned[jnp.argsort(send_order)]


def solution(mesh):
    in_specs = (
        P(("dp", "ctx"), "tp"),
        P(("dp", "ctx"), "tp"),
        P(("dp", "ctx"), "tp"),
        P(("dp", "ctx")),
        P(("dp", "ctx")),
        P("dp"),
    )
    out_specs = P(("dp", "ctx"), "tp")
    return jax.shard_map(
        on_device, mesh=mesh, in_specs=in_specs, out_specs=out_specs, check_vma=False
    )
```

profile of v0, /device:TPU:1, one launch (start us, length us, event | category | flops | bytes accessed | tf_op | source)
XLA Modules:
  0.0 314.1 jit_solution(12895272683233479751)
XLA Ops:
  12.1 10.6 %all-to-all-start.1 = ((s32[32,4,1]{1,2,0:T(1,128)}), s32[32,4,1]{1,2,0:T(1,128)S(1)}, u32[]{:S(2)}, u32[]{:S(2)}) async-start(s32[32,4,1]{1,2,0:T(1,128)} %bitcast), calls=%async_computation.1 | async-start | bytes 32768 | tf_op jit(solution)/shard_map/all_to_all | solution.py:118
  26.6 3.9 %all-to-all-done.1 = s32[32,4,1]{1,2,0:T(1,128)S(1)} async-done(((s32[32,4,1]{1,2,0:T(1,128)}), s32[32,4,1]{1,2,0:T(1,128)S(1)}, u32[]{:S(2)}, u32[]{:S(2)}) %all-to-all-start.1) | async-done | bytes 544 | tf_op jit(solution)/shard_map/all_to_all | solution.py:118
  30.5 4.4 %all-to-all-start = ((bf16[32,4,256]{2,1,0:T(4,128)(2,1)}), bf16[32,4,256]{2,1,0:T(4,128)(2,1)S(1)}, u32[]{:S(2)}, u32[]{:S(2)}) async-start(bf16[32,4,256]{2,1,0:T(4,128)(2,1)} %all_to_all.40), calls=%async_computation | async-start | bytes 131072 | tf_op jit(solution)/shard_map/all_to_all | solution.py:116
  39.0 4.2 %all-to-all-done = bf16[32,4,256]{2,1,0:T(4,128)(2,1)S(1)} async-done(((bf16[32,4,256]{2,1,0:T(4,128)(2,1)}), bf16[32,4,256]{2,1,0:T(4,128)(2,1)S(1)}, u32[]{:S(2)}, u32[]{:S(2)}) %all-to-all-start) | async-done | bytes 65568 | tf_op jit(solution)/shard_map/all_to_all | solution.py:116
  45.7 12.2 %all_to_all.60 = bf16[32,4,256]{2,1,0:T(4,128)(2,1)S(1)} all-to-all(bf16[32,4,256]{2,1,0:T(4,128)(2,1)S(1)} %all_to_all.49), channel_id=1, replica_groups=mesh['ctx'=32,'tp'=4,'dp'=4] {'ctx'}, dimensions={0} | all-to-all | bytes 131072 | tf_op jit(solution)/shard_map/all_to_all | solution.py:117
  62.6 3.9 %all-to-all-start.2 = ((bf16[32,4,2048]{2,1,0:T(4,128)(2,1)}), bf16[32,4,2048]{2,1,0:T(4,128)(2,1)S(1)}, u32[]{:S(2)}, u32[]{:S(2)}) async-start(bf16[32,4,2048]{2,1,0:T(4,128)(2,1)} %all_to_all.46), calls=%async_computation.2 | async-start | bytes 1048576 | tf_op jit(solution)/shard_map/all_to_all | solution.py:115
  69.3 15.9 %all-to-all-done.2 = bf16[32,4,2048]{2,1,0:T(4,128)(2,1)S(1)} async-done(((bf16[32,4,2048]{2,1,0:T(4,128)(2,1)}), bf16[32,4,2048]{2,1,0:T(4,128)(2,1)S(1)}, u32[]{:S(2)}, u32[]{:S(2)}) %all-to-all-start.2) | async-done | bytes 524320 | tf_op jit(solution)/shard_map/all_to_all | solution.py:115
  86.6 27.7 %all-gather.5.cloned.1.call-done = bf16[4096,256]{1,0:T(8,128)(2,1)} async-done(((bf16[128,256]{1,0:T(8,128)(2,1)}), bf16[4096,256]{1,0:T(8,128)(2,1)}) %all-gather.5.cloned.1.call-update) | async-done | bytes 2097168 | tf_op jit(solution)/shard_map/all_gather | solution.py:128
  116.8 66.3 %all-gather.7.cloned.1.call-done = bf16[4096,256]{1,0:T(8,128)(2,1)} async-done(((bf16[128,256]{1,0:T(8,128)(2,1)}), bf16[4096,256]{1,0:T(8,128)(2,1)}) %all-gather.7.cloned.1.call-update) | async-done | bytes 2097168 | tf_op jit(solution)/shard_map/all_gather | solution.py:129
  183.1 4.0 %reshape.130 = bf16[8,512,2,128]{3,2,1,0:T(2,128)(2,1)} reshape(bf16[4096,256]{1,0:T(8,128)(2,1)} %all-gather.7.cloned.1.call-done) | data formatting | bytes 4194304 | tf_op jit(solution)/shard_map/reshape | solution.py:50
  187.1 90.9 %while.17 = (s32[]{:T(128)}, f32[2,8,128]{2,1,0:T(8,128)S(1)}, f32[2,8,128]{2,1,0:T(8,128)S(1)}, f32[2,8,128,128]{3,2,1,0:T(8,128)}, s32[128]{0:T(128)S(1)}, /*i...) while((s32[]{:T(128)}, f32[2,8,128]{2,1,0:T(8,128)S(1)}, ...), condition=%wide.region_7.8_spmd.clone, body=%wide.region_3.7_spmd.clone.sunk | while | flops 553618688 | bytes 33965820 | solution.py:75
  188.7 2.7 fusion.25
  191.4 3.3 %convert_reduce_fusion.6 = f32[2,8,128]{2,1,0:T(8,128)S(1)} fusion(f32[2,8,128]{2,1,0:T(8,128)S(1)} %select_maximum_fusion.2, f32[2,512,128,8]{2,1,3,0:T(8,128)} %get-tuple-element.361, pred[128,512]{0,1:T(8,128)(4,1)S(1)} %compare_and_fusion.2), kind=kLoop, calls=%fused_computation.11.clone.1 | loop fusion | flops 7337984 | bytes 4276224 | tf_op jit(solution)/shard_map/while/body/eval_jaxpr/reduce_sum | solution.py:68
  199.0 2.7 fusion.25
  201.7 3.3 %convert_reduce_fusion.6 = f32[2,8,128]{2,1,0:T(8,128)S(1)} fusion(f32[2,8,128]{2,1,0:T(8,128)S(1)} %select_maximum_fusion.2, f32[2,512,128,8]{2,1,3,0:T(8,128)} %get-tuple-element.361, pred[128,512]{0,1:T(8,128)(4,1)S(1)} %compare_and_fusion.2), kind=kLoop, calls=%fused_computation.11.clone.1 | loop fusion | flops 7337984 | bytes 4276224 | tf_op jit(solution)/shard_map/while/body/eval_jaxpr/reduce_sum | solution.py:68
  205.1 3.8 %convolution_add_fusion.2 = f32[2,8,128,128]{3,2,1,0:T(8,128)} fusion(f32[2,8,128,128]{3,2,1,0:T(8,128)} %get-tuple-element.382, f32[2,8,128]{2,1,0:T(8,128)S(1)} %get-tuple-element.363, pred[]{:T(512)S(6)} %compare.29, bf16[1,512,2,128]{3,2,1,0:T(2,128)(2,1)S(1)} %get-tuple-element.364, f32[2,512,128,8]{2,1,3,0:T(8,128)S(1)} %copy-done.1, ...), kind=kOutput, calls=%fused_computation.14.clone.1 | convolution fusion | flops 274464768 | bytes 6635521 | tf_op jit(solution)/shard_map/while/body/eval_jaxpr/gjtk,kgd->gjtd/dot_general | solution.py:69
  213.2 3.3 %convert_reduce_fusion.6 = f32[2,8,128]{2,1,0:T(8,128)S(1)} fusion(f32[2,8,128]{2,1,0:T(8,128)S(1)} %select_maximum_fusion.2, f32[2,512,128,8]{2,1,3,0:T(8,128)} %get-tuple-element.361, pred[128,512]{0,1:T(8,128)(4,1)S(1)} %compare_and_fusion.2), kind=kLoop, calls=%fused_computation.11.clone.1 | loop fusion | flops 7337984 | bytes 4276224 | tf_op jit(solution)/shard_map/while/body/eval_jaxpr/reduce_sum | solution.py:68
  216.7 3.8 %convolution_add_fusion.2 = f32[2,8,128,128]{3,2,1,0:T(8,128)} fusion(f32[2,8,128,128]{3,2,1,0:T(8,128)} %get-tuple-element.382, f32[2,8,128]{2,1,0:T(8,128)S(1)} %get-tuple-element.363, pred[]{:T(512)S(6)} %compare.29, bf16[1,512,2,128]{3,2,1,0:T(2,128)(2,1)S(1)} %get-tuple-element.364, f32[2,512,128,8]{2,1,3,0:T(8,128)S(1)} %copy-done.1, ...), kind=kOutput, calls=%fused_computation.14.clone.1 | convolution fusion | flops 274464768 | bytes 6635521 | tf_op jit(solution)/shard_map/while/body/eval_jaxpr/gjtk,kgd->gjtd/dot_general | solution.py:69
  222.1 2.7 fusion.25
  224.7 3.3 %convert_reduce_fusion.6 = f32[2,8,128]{2,1,0:T(8,128)S(1)} fusion(f32[2,8,128]{2,1,0:T(8,128)S(1)} %select_maximum_fusion.2, f32[2,512,128,8]{2,1,3,0:T(8,128)} %get-tuple-element.361, pred[128,512]{0,1:T(8,128)(4,1)S(1)} %compare_and_fusion.2), kind=kLoop, calls=%fused_computation.11.clone.1 | loop fusion | flops 7337984 | bytes 4276224 | tf_op jit(solution)/shard_map/while/body/eval_jaxpr/reduce_sum | solution.py:68
  228.2 3.8 %convolution_add_fusion.2 = f32[2,8,128,128]{3,2,1,0:T(8,128)} fusion(f32[2,8,128,128]{3,2,1,0:T(8,128)} %get-tuple-element.382, f32[2,8,128]{2,1,0:T(8,128)S(1)} %get-tuple-element.363, pred[]{:T(512)S(6)} %compare.29, bf16[1,512,2,128]{3,2,1,0:T(2,128)(2,1)S(1)} %get-tuple-element.364, f32[2,512,128,8]{2,1,3,0:T(8,128)S(1)} %copy-done.1, ...), kind=kOutput, calls=%fused_computation.14.clone.1 | convolution fusion | flops 274464768 | bytes 6635521 | tf_op jit(solution)/shard_map/while/body/eval_jaxpr/gjtk,kgd->gjtd/dot_general | solution.py:69
  233.6 2.7 fusion.25
  236.3 3.3 %convert_reduce_fusion.6 = f32[2,8,128]{2,1,0:T(8,128)S(1)} fusion(f32[2,8,128]{2,1,0:T(8,128)S(1)} %select_maximum_fusion.2, f32[2,512,128,8]{2,1,3,0:T(8,128)} %get-tuple-element.361, pred[128,512]{0,1:T(8,128)(4,1)S(1)} %compare_and_fusion.2), kind=kLoop, calls=%fused_computation.11.clone.1 | loop fusion | flops 7337984 | bytes 4276224 | tf_op jit(solution)/shard_map/while/body/eval_jaxpr/reduce_sum | solution.py:68
  239.7 3.8 %convolution_add_fusion.2 = f32[2,8,128,128]{3,2,1,0:T(8,128)} fusion(f32[2,8,128,128]{3,2,1,0:T(8,128)} %get-tuple-element.382, f32[2,8,128]{2,1,0:T(8,128)S(1)} %get-tuple-element.363, pred[]{:T(512)S(6)} %compare.29, bf16[1,512,2,128]{3,2,1,0:T(2,128)(2,1)S(1)} %get-tuple-element.364, f32[2,512,128,8]{2,1,3,0:T(8,128)S(1)} %copy-done.1, ...), kind=kOutput, calls=%fused_computation.14.clone.1 | convolution fusion | flops 274464768 | bytes 6635521 | tf_op jit(solution)/shard_map/while/body/eval_jaxpr/gjtk,kgd->gjtd/dot_general | solution.py:69
  247.8 3.3 %convert_reduce_fusion.6 = f32[2,8,128]{2,1,0:T(8,128)S(1)} fusion(f32[2,8,128]{2,1,0:T(8,128)S(1)} %select_maximum_fusion.2, f32[2,512,128,8]{2,1,3,0:T(8,128)} %get-tuple-element.361, pred[128,512]{0,1:T(8,128)(4,1)S(1)} %compare_and_fusion.2), kind=kLoop, calls=%fused_computation.11.clone.1 | loop fusion | flops 7337984 | bytes 4276224 | tf_op jit(solution)/shard_map/while/body/eval_jaxpr/reduce_sum | solution.py:68
  251.2 3.8 %convolution_add_fusion.2 = f32[2,8,128,128]{3,2,1,0:T(8,128)} fusion(f32[2,8,128,128]{3,2,1,0:T(8,128)} %get-tuple-element.382, f32[2,8,128]{2,1,0:T(8,128)S(1)} %get-tuple-element.363, pred[]{:T(512)S(6)} %compare.29, bf16[1,512,2,128]{3,2,1,0:T(2,128)(2,1)S(1)} %get-tuple-element.364, f32[2,512,128,8]{2,1,3,0:T(8,128)S(1)} %copy-done.1, ...), kind=kOutput, calls=%fused_computation.14.clone.1 | convolution fusion | flops 274464768 | bytes 6635521 | tf_op jit(solution)/shard_map/while/body/eval_jaxpr/gjtk,kgd->gjtd/dot_general | solution.py:69
  259.3 3.3 %convert_reduce_fusion.6 = f32[2,8,128]{2,1,0:T(8,128)S(1)} fusion(f32[2,8,128]{2,1,0:T(8,128)S(1)} %select_maximum_fusion.2, f32[2,512,128,8]{2,1,3,0:T(8,128)} %get-tuple-element.361, pred[128,512]{0,1:T(8,128)(4,1)S(1)} %compare_and_fusion.2), kind=kLoop, calls=%fused_computation.11.clone.1 | loop fusion | flops 7337984 | bytes 4276224 | tf_op jit(solution)/shard_map/while/body/eval_jaxpr/reduce_sum | solution.py:68
  262.7 3.8 %convolution_add_fusion.2 = f32[2,8,128,128]{3,2,1,0:T(8,128)} fusion(f32[2,8,128,128]{3,2,1,0:T(8,128)} %get-tuple-element.382, f32[2,8,128]{2,1,0:T(8,128)S(1)} %get-tuple-element.363, pred[]{:T(512)S(6)} %compare.29, bf16[1,512,2,128]{3,2,1,0:T(2,128)(2,1)S(1)} %get-tuple-element.364, f32[2,512,128,8]{2,1,3,0:T(8,128)S(1)} %copy-done.1, ...), kind=kOutput, calls=%fused_computation.14.clone.1 | convolution fusion | flops 274464768 | bytes 6635521 | tf_op jit(solution)/shard_map/while/body/eval_jaxpr/gjtk,kgd->gjtd/dot_general | solution.py:69
  270.8 3.3 %convert_reduce_fusion.6 = f32[2,8,128]{2,1,0:T(8,128)S(1)} fusion(f32[2,8,128]{2,1,0:T(8,128)S(1)} %select_maximum_fusion.2, f32[2,512,128,8]{2,1,3,0:T(8,128)} %get-tuple-element.361, pred[128,512]{0,1:T(8,128)(4,1)S(1)} %compare_and_fusion.2), kind=kLoop, calls=%fused_computation.11.clone.1 | loop fusion | flops 7337984 | bytes 4276224 | tf_op jit(solution)/shard_map/while/body/eval_jaxpr/reduce_sum | solution.py:68
  274.3 3.8 %convolution_add_fusion.2 = f32[2,8,128,128]{3,2,1,0:T(8,128)} fusion(f32[2,8,128,128]{3,2,1,0:T(8,128)} %get-tuple-element.382, f32[2,8,128]{2,1,0:T(8,128)S(1)} %get-tuple-element.363, pred[]{:T(512)S(6)} %compare.29, bf16[1,512,2,128]{3,2,1,0:T(2,128)(2,1)S(1)} %get-tuple-element.364, f32[2,512,128,8]{2,1,3,0:T(8,128)S(1)} %copy-done.1, ...), kind=kOutput, calls=%fused_computation.14.clone.1 | convolution fusion | flops 274464768 | bytes 6635521 | tf_op jit(solution)/shard_map/while/body/eval_jaxpr/gjtk,kgd->gjtd/dot_general | solution.py:69
  282.0 6.7 %all-to-all-start.4 = ((bf16[32,4,2048]{2,1,0:T(4,128)(2,1)}), bf16[32,4,2048]{2,1,0:T(4,128)(2,1)S(1)}, u32[]{:S(2)}, u32[]{:S(2)}) async-start(bf16[32,4,2048]{2,1,0:T(4,128)(2,1)} %all_to_all.52), calls=%async_computation.4 | async-start | bytes 1048576 | tf_op jit(solution)/shard_map/all_to_all | solution.py:138
  291.4 14.1 %all-to-all-done.4 = bf16[32,4,2048]{2,1,0:T(4,128)(2,1)S(1)} async-done(((bf16[32,4,2048]{2,1,0:T(4,128)(2,1)}), bf16[32,4,2048]{2,1,0:T(4,128)(2,1)S(1)}, u32[]{:S(2)}, u32[]{:S(2)}) %all-to-all-start.4) | async-done | bytes 524320 | tf_op jit(solution)/shard_map/all_to_all | solution.py:138
  (166 shorter events, 62.8 us)
Async XLA Ops:
  6.5 38.2 %copy-start = (bf16[128,256]{1,0:T(8,128)(2,1)S(1)}, bf16[128,256]{1,0:T(8,128)(2,1)}, u32[]{:S(2)}) copy-start(bf16[128,256]{1,0:T(8,128)(2,1)} %param.10) | copy-start | bytes 196612
  6.5 52.8 %copy-start.2 = (bf16[128,2048]{1,0:T(8,128)(2,1)S(1)}, bf16[128,2048]{1,0:T(8,128)(2,1)}, u32[]{:S(2)}) copy-start(bf16[128,2048]{1,0:T(8,128)(2,1)} %param.8) | copy-start | bytes 1572868
  12.1 18.4 %all-to-all-start.1 = ((s32[32,4,1]{1,2,0:T(1,128)}), s32[32,4,1]{1,2,0:T(1,128)S(1)}, u32[]{:S(2)}, u32[]{:S(2)}) async-start(s32[32,4,1]{1,2,0:T(1,128)} %bitcast), calls=%async_computation.1 | async-start | bytes 32768 | tf_op jit(solution)/shard_map/all_to_all | solution.py:118
  30.5 12.7 %all-to-all-start = ((bf16[32,4,256]{2,1,0:T(4,128)(2,1)}), bf16[32,4,256]{2,1,0:T(4,128)(2,1)S(1)}, u32[]{:S(2)}, u32[]{:S(2)}) async-start(bf16[32,4,256]{2,1,0:T(4,128)(2,1)} %all_to_all.40), calls=%async_computation | async-start | bytes 131072 | tf_op jit(solution)/shard_map/all_to_all | solution.py:116
  34.9 79.4 %all-gather.5.cloned.1.call-start = ((), (), s32[]{:S(2)}) async-start(), calls=%async_computation.5 | async-start | bytes 2162688 | tf_op jit(solution)/shard_map/all_gather | solution.py:128
  44.7 138.4 %all-gather.7.cloned.1.call-start = ((), (), s32[]{:S(2)}) async-start(), calls=%async_computation.6 | async-start | bytes 2162688 | tf_op jit(solution)/shard_map/all_gather | solution.py:129
  60.5 6.1 %copy-start.3 = (s32[16]{0:T(128)S(1)}, s32[16]{0:T(128)}, u32[]{:S(2)}) copy-start(s32[16]{0:T(128)} %param.13) | copy-start | bytes 196
  62.6 22.6 %all-to-all-start.2 = ((bf16[32,4,2048]{2,1,0:T(4,128)(2,1)}), bf16[32,4,2048]{2,1,0:T(4,128)(2,1)S(1)}, u32[]{:S(2)}, u32[]{:S(2)}) async-start(bf16[32,4,2048]{2,1,0:T(4,128)(2,1)} %all_to_all.46), calls=%async_computation.2 | async-start | bytes 1048576 | tf_op jit(solution)/shard_map/all_to_all | solution.py:115
  191.4 3.4 %copy-start.1 = (f32[2,512,128,8]{2,1,3,0:T(8,128)S(1)}, f32[2,512,128,8]{2,1,3,0:T(8,128)}, u32[]{:S(2)}) copy-start(f32[2,512,128,8]{2,1,3,0:T(8,128)} %get-tuple-element.361) | copy-start | bytes 12582916 | tf_op jit(solution)/shard_map/while
  201.7 3.4 %copy-start.1 = (f32[2,512,128,8]{2,1,3,0:T(8,128)S(1)}, f32[2,512,128,8]{2,1,3,0:T(8,128)}, u32[]{:S(2)}) copy-start(f32[2,512,128,8]{2,1,3,0:T(8,128)} %get-tuple-element.361) | copy-start | bytes 12582916 | tf_op jit(solution)/shard_map/while
  213.2 3.4 %copy-start.1 = (f32[2,512,128,8]{2,1,3,0:T(8,128)S(1)}, f32[2,512,128,8]{2,1,3,0:T(8,128)}, u32[]{:S(2)}) copy-start(f32[2,512,128,8]{2,1,3,0:T(8,128)} %get-tuple-element.361) | copy-start | bytes 12582916 | tf_op jit(solution)/shard_map/while
  224.7 3.4 %copy-start.1 = (f32[2,512,128,8]{2,1,3,0:T(8,128)S(1)}, f32[2,512,128,8]{2,1,3,0:T(8,128)}, u32[]{:S(2)}) copy-start(f32[2,512,128,8]{2,1,3,0:T(8,128)} %get-tuple-element.361) | copy-start | bytes 12582916 | tf_op jit(solution)/shard_map/while
  236.3 3.4 %copy-start.1 = (f32[2,512,128,8]{2,1,3,0:T(8,128)S(1)}, f32[2,512,128,8]{2,1,3,0:T(8,128)}, u32[]{:S(2)}) copy-start(f32[2,512,128,8]{2,1,3,0:T(8,128)} %get-tuple-element.361) | copy-start | bytes 12582916 | tf_op jit(solution)/shard_map/while
  247.8 3.4 %copy-start.1 = (f32[2,512,128,8]{2,1,3,0:T(8,128)S(1)}, f32[2,512,128,8]{2,1,3,0:T(8,128)}, u32[]{:S(2)}) copy-start(f32[2,512,128,8]{2,1,3,0:T(8,128)} %get-tuple-element.361) | copy-start | bytes 12582916 | tf_op jit(solution)/shard_map/while
  259.3 3.4 %copy-start.1 = (f32[2,512,128,8]{2,1,3,0:T(8,128)S(1)}, f32[2,512,128,8]{2,1,3,0:T(8,128)}, u32[]{:S(2)}) copy-start(f32[2,512,128,8]{2,1,3,0:T(8,128)} %get-tuple-element.361) | copy-start | bytes 12582916 | tf_op jit(solution)/shard_map/while
  270.8 3.4 %copy-start.1 = (f32[2,512,128,8]{2,1,3,0:T(8,128)S(1)}, f32[2,512,128,8]{2,1,3,0:T(8,128)}, u32[]{:S(2)}) copy-start(f32[2,512,128,8]{2,1,3,0:T(8,128)} %get-tuple-element.361) | copy-start | bytes 12582916 | tf_op jit(solution)/shard_map/while
  282.0 23.4 %all-to-all-start.4 = ((bf16[32,4,2048]{2,1,0:T(4,128)(2,1)}), bf16[32,4,2048]{2,1,0:T(4,128)(2,1)S(1)}, u32[]{:S(2)}, u32[]{:S(2)}) async-start(bf16[32,4,2048]{2,1,0:T(4,128)(2,1)} %all_to_all.52), calls=%async_computation.4 | async-start | bytes 1048576 | tf_op jit(solution)/shard_map/all_to_all | solution.py:138
Sparse Core Ops, SparseCore 0:
  44.8 69.3 all-gather.4
  116.4 66.6 all-gather.6
where the time goes:
time: 315 us; the launch traced here: 314 us
  waiting for transfers between devices  132 us (42%)
  matrix products  50.2 us (16%)
  other arithmetic  45 us (14%)
  local copies, waits for them, and re-layouts  35 us (11%)
  starting transfers between devices  25.7 us (8%)
  between operations  13.7 us (4%)
  blocking collectives  12.2 us (4%)
    all_gather x1, waiting for transfers between devices, on_device(): lax.all_gather(v_local, 'ctx', axis=0, tiled=True)  66.3 us
    dot_general x8, matrix products, one_step(): jnp.einsum('gjtk,kgd->gjtd', weights, value_block, preferred_element_type...  28.9 us
    all_gather x1, waiting for transfers between devices, on_device(): lax.all_gather(k_local, 'ctx', axis=0, tiled=True)  27.7 us
    reduce_sum x8, other arithmetic, one_step(): totals = totals * rescale + jnp.sum(weights, axis=-1, dtype=jnp.float32)  26.6 us
    dot_general x8, matrix products, one_step(): jnp.einsum('tgjd,kgd->gjtk', query_grouped, key_block, preferred_element_...  21.3 us
    all_to_all x1, waiting for transfers between devices, on_device(): lax.all_to_all(outgoing[0], 'ctx', split_axis=0, concat_axis=0, tiled=True)  15.9 us
    all_to_all x1, waiting for transfers between devices, on_device(): lax.all_to_all(back_rows, 'ctx', split_axis=0, concat_axis=0, tiled=True)  14.1 us
    all_to_all x1, blocking collectives, on_device(): lax.all_to_all(outgoing[2], 'ctx', split_axis=0, concat_axis=0, tiled=True)  12.2 us
  transfers between devices with their start and end apart: 6, of which 6 were waited for; matrix products, arithmetic and copies ran while one was open for 7% of the time, Pallas kernels for 0%

commit v1 on v0

v1 whole, which is shorter than its diff:
```python
import functools
import math

import jax
import jax.numpy as jnp
import numpy as np
from jax import lax
from jax.experimental import pallas as pl
from jax.experimental.pallas import tpu as pltpu
from jax.sharding import PartitionSpec as P

MESH = pl.DeviceIdType.MESH
HEAD_WIDTH = 128
HALF = HEAD_WIDTH // 2
ROPE_BASE = 1000000.0
SCALE = math.log2(math.e) / math.sqrt(HEAD_WIDTH)
ROWS = 128
GROUP = 8
COLS = GROUP * ROWS
NY = 8
UNIT = 512
MASKED = -1e30
SUB_ROWS = ((0, 256), (256, 272))
ITEM_ROWS = 528

PLAN = {
    "edges": [
        (0, (0, 1), (0, 0)), (0, (1, 0), (0, 0)), (0, (-1, 0), (0, 0)), (0, (1, 1), (1, 0)), (0, (-1, 1), (-1, 0)),
        (0, (2, 0), (1, 0)), (0, (-2, 0), (-1, 0)), (0, (2, 1), (2, 0)), (0, (-2, 1), (-2, 0)), (0, (3, 0), (2, 0)),
        (0, (-3, 0), (-2, 0)), (0, (3, 1), (3, 0)), (0, (-3, 1), (-3, 0)), (0, (4, 0), (3, 0)), (0, (4, 1), (3, 1)),
        (1, (0, 1), (0, 0)), (1, (1, 0), (0, 0)), (1, (-1, 0), (0, 0)), (1, (1, 1), (0, 1)), (1, (-1, 1), (0, 1)),
        (1, (2, 0), (1, 0)), (1, (-2, 0), (-1, 0)), (1, (2, 1), (1, 1)), (1, (-2, 1), (-1, 1)), (1, (3, 0), (2, 0)),
        (1, (-3, 0), (-2, 0)), (1, (3, 1), (2, 1)), (1, (-3, 1), (-2, 1)), (1, (-4, 0), (-3, 0)),
        (1, (-4, 1), (-4, 0)),
    ],
    "waits": [
        (0, (0, 1)), (0, (1, 0)), (0, (-1, 0)), (1, (0, 1)), (1, (1, 0)), (1, (-1, 0)), (0, (1, 1)), (0, (2, 0)),
        (0, (-2, 0)), (0, (-1, 1)), (1, (1, 1)), (1, (-2, 0)), (1, (-1, 1)), (1, (2, 0)), (0, (2, 1)), (0, (-2, 1)),
        (0, (-3, 0)), (0, (3, 0)), (1, (2, 1)), (1, (-3, 0)), (1, (-2, 1)), (1, (3, 0)), (0, (-3, 1)), (0, (3, 1)),
        (0, (4, 0)), (1, (-4, 0)), (1, (3, 1)), (1, (-3, 1)), (0, (4, 1)), (1, (-4, 1)),
    ],
    "steps": [
        [(0, 0)], [(0, 1), (1, 0)], [(-1, 0), (1, 1)], [(-2, 0), (-1, 1)], [(2, 0), (2, 1)], [(-3, 0), (-2, 1)],
        [(3, 0), (4, 0)], [(3, 1), (-3, 1)], [(4, 1)],
    ],
    "before": [
        0, 0, 0, 0, 6, 6, 6, 6, 11, 11, 12, 14, 16, 18, 18, 18, 19, 20, 22, 22, 25, 25, 25, 27, 28, 28, 28, 29, 29,
        29, 30, 30, 30, 30, 30, 30,
    ],
}


def sine_cosine(angle):
    turn = jnp.floor(angle * (2.0 / math.pi) + 0.5)
    rest = ((angle - turn * 1.5703125) - turn * 4.837512969970703125e-4) - turn * 7.54978995489188216e-8
    square = rest * rest
    sine = ((-1.9515295891e-4 * square + 8.3321608736e-3) * square - 1.6666654611e-1) * square * rest + rest
    cosine = (
        (2.443315711809948e-5 * square - 1.388731625493765e-3) * square + 4.166664568298827e-2
    ) * square * square - 0.5 * square + 1.0
    quarter = turn.astype(jnp.int32)
    swap = (quarter & 1) == 1
    sine_out = jnp.where(swap, cosine, sine)
    cosine_out = jnp.where(swap, sine, cosine)
    sine_out = jnp.where((quarter & 2) == 2, -sine_out, sine_out)
    cosine_out = jnp.where(((quarter + 1) & 2) == 2, -cosine_out, cosine_out)
    return sine_out, cosine_out


def kernel(
    q_hbm, k_hbm, v_hbm, pos_hbm, reset_hbm, freq_hbm, out_hbm,
    q_in, k_in, v_in, pos_in, reset_in, freq_in,
    items, stage, q_t, q_stage, place, place_sib, bounds, mask, top, total, acc, out_buf,
    in_sem, item_sem, sib_sem, send_sem, out_sem,
):
    ctx = lax.axis_index("ctx")
    tp = lax.axis_index("tp")
    dp = lax.axis_index("dp")
    y, z, core = ctx // 4, (ctx // 2) % 2, ctx % 2

    def device(yy, zz, cc):
        return ((yy * 2 + zz) * 2 + cc, tp, dp)

    def around(yy):
        return lax.rem(yy + 2 * NY, NY)

    sibling = device(y, z, 1 - core)

    barrier = pltpu.get_barrier_semaphore()
    for other in (
        device(around(y + 1), z, core), device(around(y - 1), z, core), device(y, 1 - z, core), sibling,
    ):
        pl.semaphore_signal(barrier, inc=1, device_id=other, device_id_type=MESH)

    def head_cols(slot, width):
        head = core if slot == 0 else 1 - core
        return pl.ds(pl.multiple_of(head * width, width), width)

    loads = [
        pltpu.make_async_copy(pos_hbm, pos_in, in_sem.at[0]),
        pltpu.make_async_copy(reset_hbm, reset_in, in_sem.at[1]),
        pltpu.make_async_copy(freq_hbm, freq_in, in_sem.at[2]),
    ]
    for slot in (1, 0):
        loads.append(pltpu.make_async_copy(k_hbm.at[:, head_cols(slot, HEAD_WIDTH)], k_in.at[slot], in_sem.at[3 + slot]))
        loads.append(pltpu.make_async_copy(v_hbm.at[:, head_cols(slot, HEAD_WIDTH)], v_in.at[slot], in_sem.at[5 + slot]))
    for slot in (1, 0):
        loads.append(pltpu.make_async_copy(q_hbm.at[:, head_cols(slot, COLS)], q_in.at[slot], in_sem.at[7 + slot]))
    for load in loads:
        load.start()

    for load in loads[:3]:
        load.wait()
    pos = pos_in[...].astype(jnp.float32)
    reset = reset_in[...].astype(jnp.float32)
    sine, cosine = sine_cosine(freq_in[...] * reset)
    sine_rows = jnp.concatenate([-sine, sine], axis=0).T
    cosine_rows = jnp.concatenate([cosine, cosine], axis=0).T
    place[...] = jnp.concatenate([pos, pos - reset, jnp.zeros((6, ROWS), jnp.float32)], axis=0)
    bounds[0] = place[...]
    sine_q, cosine_q = sine * SCALE, cosine * SCALE

    my_slot = y * 2 + z
    for load in loads[3:7]:
        load.wait()

    def keys_of(slot):
        raw = k_in[slot].astype(jnp.float32)
        return (raw * cosine_rows + pltpu.roll(raw, HALF, 1) * sine_rows).astype(jnp.bfloat16)

    def values_of(slot):
        return v_in[slot].astype(jnp.float32).T.astype(jnp.bfloat16)

    stage[0:ROWS] = keys_of(1)
    stage[ROWS : 2 * ROWS] = values_of(1)
    items[my_slot, 0:ROWS] = keys_of(0)
    items[my_slot, ROWS : 2 * ROWS] = values_of(0)

    pl.semaphore_wait(barrier, 4)

    to_sibling = [
        pltpu.make_async_remote_copy(
            src_ref=place, dst_ref=place_sib, send_sem=sib_sem.at[0], recv_sem=sib_sem.at[1],
            device_id=sibling, device_id_type=MESH,
        ),
        pltpu.make_async_remote_copy(
            src_ref=stage, dst_ref=items.at[my_slot, pl.ds(256, 256)], send_sem=sib_sem.at[2],
            recv_sem=sib_sem.at[3], device_id=sibling, device_id_type=MESH,
        ),
        pltpu.make_async_remote_copy(
            src_ref=q_stage, dst_ref=q_t.at[pl.ds(0, HEAD_WIDTH), pl.ds(COLS, COLS)], send_sem=sib_sem.at[4],
            recv_sem=sib_sem.at[5], device_id=sibling, device_id_type=MESH,
        ),
    ]

    def part_copy(sub, slot, target):
        rows = items.at[slot, pl.ds(*SUB_ROWS[sub])]
        return pltpu.make_async_remote_copy(
            src_ref=rows, dst_ref=rows, send_sem=send_sem, recv_sem=item_sem.at[sub, slot],
            device_id=target, device_id_type=MESH,
        )

    children = {}
    for sub, node, parent in PLAN["edges"]:
        children.setdefault((sub, parent), []).append(node)

    def slot_of(node):
        return around(y - node[0]) * 2 + (z if node[1] == 0 else 1 - z)

    def hand_on(sub, node):
        for child in children.get((sub, node), []):
            target = device(around(y + child[0] - node[0]), z if child[1] == node[1] else 1 - z, core)
            part_copy(sub, slot_of(node), target).start()

    def receive(sub, node):
        part_copy(sub, slot_of(node), sibling).wait_recv()
        hand_on(sub, node)

    def rotate_queries(slot):
        for head in range(GROUP):
            cols = slice(head * ROWS, (head + 1) * ROWS)
            raw = q_in[slot, :, cols].astype(jnp.float32).T
            low, high = raw[:HALF], raw[HALF:]
            turned = jnp.concatenate(
                [low * cosine_q - high * sine_q, high * cosine_q + low * sine_q], axis=0
            ).astype(jnp.bfloat16)
            if slot == 0:
                q_t[0:HEAD_WIDTH, cols] = turned
            else:
                q_stage[:, cols] = turned

    to_sibling[0].start()
    to_sibling[1].start()
    hand_on(0, (0, 0))

    loads[7].wait()
    rotate_queries(1)
    to_sibling[2].start()

    to_sibling[0].wait_recv()
    bounds[1] = place_sib[...]
    place_rows = []
    for group in range(2):
        at = bounds[group, 0:1]
        high = jnp.floor(at * (1.0 / 64.0))
        place_rows += [high, at - high * 64.0]
    items[my_slot, 512:528] = jnp.concatenate(
        place_rows + [jnp.zeros((12, ROWS), jnp.float32)], axis=0
    ).astype(jnp.bfloat16)
    to_sibling[1].wait_recv()
    hand_on(1, (0, 0))

    loads[8].wait()
    rotate_queries(0)
    unit_matrix = (
        lax.broadcasted_iota(jnp.int32, (ROWS, ROWS), 0) == lax.broadcasted_iota(jnp.int32, (ROWS, ROWS), 1)
    ).astype(jnp.float32).astype(jnp.bfloat16)
    for head in range(2 * GROUP):
        q_t[HEAD_WIDTH:, head * ROWS : (head + 1) * ROWS] = unit_matrix
    top[...] = jnp.full_like(top, MASKED)
    total[...] = jnp.zeros_like(total)
    acc[...] = jnp.zeros_like(acc)
    to_sibling[2].wait_recv()

    steps = PLAN["steps"]
    units = [(step, unit) for step in range(len(steps)) for unit in range(2 * COLS // UNIT)]

    def prepare(step):
        row = 0
        for node in steps[step]:
            slot = slot_of(node)
            tile = items[slot, 512:528].astype(jnp.float32)
            for part in range(2):
                at = tile[2 * part : 2 * part + 1] * 64.0 + tile[2 * part + 1 : 2 * part + 2]
                at = jnp.broadcast_to(at, (ROWS, ROWS)).T
                for group in range(2):
                    seen = (at <= bounds[group, 0:1]) & (at >= bounds[group, 1:2])
                    mask[step % 2, group, row : row + ROWS] = jnp.where(seen, 0.0, MASKED).astype(jnp.bfloat16)
                row += ROWS

    def score(step, unit):
        group = unit * UNIT // COLS
        keys = []
        for node in steps[step]:
            slot = slot_of(node)
            keys += [items[slot, 0:ROWS], items[slot, 256 : 256 + ROWS]]
        keys = jnp.concatenate(keys, axis=0)
        left = jnp.concatenate([keys, mask[step % 2, group, : keys.shape[0]]], axis=1)
        return jnp.dot(left, q_t[:, unit * UNIT : (unit + 1) * UNIT], preferred_element_type=jnp.float32)

    def weigh(unit, scores):
        cols = slice(unit * UNIT, (unit + 1) * UNIT)
        before = top[:, cols]
        now = jnp.maximum(before, jnp.max(scores, axis=0, keepdims=True))
        rescale = jnp.exp2(before - now)
        top[:, cols] = now
        weights = jnp.exp2(scores - now)
        total[:, cols] = total[:, cols] * rescale + jnp.sum(weights, axis=0, keepdims=True)
        return weights.astype(jnp.bfloat16), rescale

    def gather_values(step, unit, weights, rescale):
        cols = slice(unit * UNIT, (unit + 1) * UNIT)
        values = []
        for node in steps[step]:
            slot = slot_of(node)
            values += [items[slot, ROWS : 2 * ROWS], items[slot, 256 + ROWS : 512]]
        values = jnp.concatenate(values, axis=1)
        acc[:, cols] = acc[:, cols] * rescale + jnp.dot(values, weights, preferred_element_type=jnp.float32)

    def finish(group):
        for head in range(GROUP):
            cols = slice(group * COLS + head * ROWS, group * COLS + (head + 1) * ROWS)
            result = acc[:, cols] / total[:, cols]
            out_buf[group, :, head * ROWS : (head + 1) * ROWS] = result.T.astype(jnp.bfloat16)

    out_cols = pl.ds(pl.multiple_of(core * COLS, COLS), COLS)
    back = pltpu.make_async_remote_copy(
        src_ref=out_buf.at[1], dst_ref=out_hbm.at[:, out_cols], send_sem=out_sem.at[0], recv_sem=out_sem.at[1],
        device_id=sibling, device_id_type=MESH,
    )
    keep = pltpu.make_async_copy(out_buf.at[0], out_hbm.at[:, out_cols], out_sem.at[2])

    waits = PLAN["waits"]
    made = 0

    def make_waits(count):
        nonlocal made
        while made < count:
            receive(*waits[made])
            made += 1

    def scores_of(index):
        make_waits(PLAN["before"][index])
        step, unit = units[index]
        if unit == UNIT_ORDER[0]:
            prepare(step)
        return score(step, unit)

    units = [(step, unit) for step in range(len(steps)) for unit in UNIT_ORDER]
    coming = scores_of(0)
    pending = None
    for index, (step, unit) in enumerate(units):
        scores = coming
        if index + 1 < len(units):
            coming = scores_of(index + 1)
        weights, rescale = weigh(unit, scores)
        if pending is not None:
            gather_values(*pending)
        pending = (step, unit, weights, rescale)
        if index == len(units) - 2:
            pass
    gather_values(*pending)
    finish(1)
    back.start()
    finish(0)
    keep.start()

    all_parts = items.at[pl.ds(0, 2 * NY - 1)]
    pltpu.make_async_copy(all_parts, all_parts, send_sem).wait()
    for copy in to_sibling:
        copy.wait_send()
    back.wait()
    keep.wait()


UNIT_ORDER = tuple(range(2 * COLS // UNIT))[::-1]


def on_device(queries, keys, values, loader_pos, reset_pos, doc_starts):
    del doc_starts
    frequency = (ROPE_BASE ** (-np.arange(HALF, dtype=np.float64) * 2.0 / HEAD_WIDTH)).astype(np.float32)
    frequency = jnp.asarray(np.broadcast_to(frequency[:, None], (HALF, ROWS)))
    bf16, f32 = jnp.bfloat16, jnp.float32
    return pl.pallas_call(
        kernel,
        out_shape=jax.ShapeDtypeStruct((ROWS, 2 * COLS), bf16),
        in_specs=[pl.BlockSpec(memory_space=pl.ANY)] * 6,
        out_specs=pl.BlockSpec(memory_space=pl.ANY),
        scratch_shapes=[
            pltpu.VMEM((2, ROWS, COLS), bf16),
            pltpu.VMEM((2, ROWS, HEAD_WIDTH), bf16),
            pltpu.VMEM((2, ROWS, HEAD_WIDTH), bf16),
            pltpu.VMEM((1, ROWS), jnp.int32),
            pltpu.VMEM((1, ROWS), jnp.int32),
            pltpu.VMEM((HALF, ROWS), f32),
            pltpu.VMEM((2 * NY, ITEM_ROWS, HEAD_WIDTH), bf16),
            pltpu.VMEM((256, HEAD_WIDTH), bf16),
            pltpu.VMEM((2 * HEAD_WIDTH, 2 * COLS), bf16),
            pltpu.VMEM((HEAD_WIDTH, COLS), bf16),
            pltpu.VMEM((8, ROWS), f32),
            pltpu.VMEM((8, ROWS), f32),
            pltpu.VMEM((2, 8, ROWS), f32),
            pltpu.VMEM((2, 2, 4 * ROWS, ROWS), bf16),
            pltpu.VMEM((1, 2 * COLS), f32),
            pltpu.VMEM((1, 2 * COLS), f32),
            pltpu.VMEM((HEAD_WIDTH, 2 * COLS), f32),
            pltpu.VMEM((2, ROWS, COLS), bf16),
            pltpu.SemaphoreType.DMA((9,)),
            pltpu.SemaphoreType.DMA((2, 2 * NY)),
            pltpu.SemaphoreType.DMA((6,)),
            pltpu.SemaphoreType.DMA,
            pltpu.SemaphoreType.DMA((3,)),
        ],
        compiler_params=pltpu.CompilerParams(
            collective_id=0, has_side_effects=True, vmem_limit_bytes=48 * 2**20
        ),
    )(queries, keys, values, loader_pos.reshape(1, ROWS), reset_pos.reshape(1, ROWS), frequency)


def solution(mesh):
    rows = ("dp", "ctx")
    return jax.shard_map(
        on_device,
        mesh=mesh,
        in_specs=(P(rows, "tp"), P(rows, "tp"), P(rows, "tp"), P(rows), P(rows), P("dp")),
        out_specs=P(rows, "tp"),
        check_vma=False,
    )
```

time: 315 us -> 39.2 us (0.12)
  waiting for transfers between devices: 132 us -> 0 us
  matrix products: 50.2 us -> 0 us
  other arithmetic: 45 us -> 0 us
  Pallas kernels: 0 us -> 34 us
  local copies, waits for them, and re-layouts: 35 us -> 4.84 us
  starting transfers between devices: 25.7 us -> 0 us
  between operations: 13.7 us -> 0.02 us
  blocking collectives: 12.2 us -> 0 us
    all_gather x2 -> x0, waiting for transfers between devices: 94 us -> none  [the longest x1 66.3 us: on_device(): lax.all_gather(v_local, 'ctx', axis=0, tiled=True)]
    dot_general x16 -> x0, matrix products: 50.2 us -> none  [the longest x8 28.9 us: one_step(): jnp.einsum('gjtk,kgd->gjtd', weights, value_block, preferred_element_type...]
    all_to_all x4 -> x0, waiting for transfers between devices: 38.1 us -> none  [the longest x1 15.9 us: on_device(): lax.all_to_all(outgoing[0], 'ctx', split_axis=0, concat_axis=0, tiled=True)]
    pallas_call x0 -> x1, Pallas kernels: none -> 34 us  [on_device(): pl.pallas_call(kernel, out_shape=jax.ShapeDtypeStruct((ROWS, 2 * COLS), b...]
    reduce_sum x17 -> x0, other arithmetic: 27.4 us -> none  [the longest x8 26.6 us: one_step(): totals = totals * rescale + jnp.sum(weights, axis=-1, dtype=jnp.float32)]
    all_to_all x4 -> x0, starting transfers between devices: 25.6 us -> none  [the longest x1 10.6 us: on_device(): lax.all_to_all(outgoing[3], 'ctx', split_axis=0, concat_axis=0, tiled=True)]
    all_to_all x1 -> x0, blocking collectives: 12.2 us -> none  [on_device(): lax.all_to_all(outgoing[2], 'ctx', split_axis=0, concat_axis=0, tiled=True)]
    gather x9 -> x0, local copies, waits for them, and re-layouts: 10.7 us -> none  [the longest x1 1.73 us: on_device(): return returned[jnp.argsort(send_order)]]
  transfers between devices with their start and end apart: 6 -> 0, of which waited for: 6 -> 0; matrix products, arithmetic and copies ran while one was open for 7% -> 0% of each run, Pallas kernels for 0% -> 0%
where the time goes in v1:
time: 39.2 us; the launch traced here: 38.9 us
  Pallas kernels  34 us (87%)
  local copies, waits for them, and re-layouts  4.84 us (12%)
    pallas_call x1, Pallas kernels, on_device(): pl.pallas_call(kernel, out_shape=jax.ShapeDtypeStruct((ROWS, 2 * COLS), b...  34 us
    unnamed x13, local copies, waits for them, and re-layouts  4.77 us

profile of v1, /device:TPU:1, one launch (start us, length us, event | category | flops | bytes accessed | tf_op | source)
XLA Modules:
  0.0 38.9 jit_solution(3192379643706381921)
XLA Ops:
  0.0 0.0 copy-start.5
  0.0 0.7 %copy-done.5 = f32[64]{0:T(128)S(1)} copy-done((f32[64]{0:T(128)S(1)}, f32[64]{0:T(128)}, u32[]{:S(2)}) %copy-start.5) | copy-done | bytes 280
  0.7 0.0 copy-start.3
  0.7 0.0 copy-start.4
  0.7 0.1 jit_solution_.3.freq_hbm
  0.7 0.6 %copy-done.3 = s32[128]{0:T(128)S(1)} copy-done((s32[128]{0:T(128)S(1)}, s32[128]{0:T(128)}, u32[]{:S(2)}) %copy-start.3) | copy-done | bytes 536
  1.3 0.0 copy-done.4
  1.3 0.0 copy-start
  1.3 1.0 %copy-done = bf16[128,2048]{1,0:T(8,128)(2,1)S(1)} copy-done((bf16[128,2048]{1,0:T(8,128)(2,1)S(1)}, bf16[128,2048]{1,0:T(8,128)(2,1)}, u32[]{:S(2)}) %copy-start) | copy-done | bytes 524312
  2.4 0.0 copy-start.1
  2.4 0.8 %copy-done.1 = bf16[128,256]{1,0:T(8,128)(2,1)S(1)} copy-done((bf16[128,256]{1,0:T(8,128)(2,1)S(1)}, bf16[128,256]{1,0:T(8,128)(2,1)}, u32[]{:S(2)}) %copy-start.1) | copy-done | bytes 65560
  3.2 0.0 copy-start.2
  3.2 0.8 %copy-done.2 = bf16[128,256]{1,0:T(8,128)(2,1)S(1)} copy-done((bf16[128,256]{1,0:T(8,128)(2,1)S(1)}, bf16[128,256]{1,0:T(8,128)(2,1)}, u32[]{:S(2)}) %copy-start.2) | copy-done | bytes 65560
  4.0 34.0 %shard_map.64 = bf16[128,2048]{1,0:T(8,128)(2,1)S(1)} custom-call(bf16[128,2048]{1,0:T(8,128)(2,1)S(1)} %copy-done, bf16[128,256]{1,0:T(8,128)(2,1)S(1)} %copy-done.1, bf16[128,256]{1,0:T(8,128)(2,1)S(1)} %copy-done.2, s32[1,128]{1,0:T(1,128)S(1)} %bitcast.2, s32[1,128]{1,0:T(1,128)S(1)} %bitcast.3, f32[64,128]{1,0:T(8,128)S(1)} %jit_solution_.3.freq_hbm), custom_call_target="tpu_custom_call" | custom-call | tf_op jit(solution)/shard_map/pallas_call | solution.py:334
  38.1 0.8 %copy.8 = bf16[128,2048]{1,0:T(8,128)(2,1)} copy(bf16[128,2048]{1,0:T(8,128)(2,1)S(1)} %shard_map.64) | data formatting | bytes 1048576
Async XLA Ops:
  0.0 0.7 %copy-start.5 = (f32[64]{0:T(128)S(1)}, f32[64]{0:T(128)}, u32[]{:S(2)}) copy-start(f32[64]{0:T(128)} %constant.2.clone) | copy-start | bytes 772
  0.7 0.7 %copy-start.3 = (s32[128]{0:T(128)S(1)}, s32[128]{0:T(128)}, u32[]{:S(2)}) copy-start(s32[128]{0:T(128)} %param.10) | copy-start | bytes 1540
  0.7 0.7 %copy-start.4 = (s32[128]{0:T(128)S(1)}, s32[128]{0:T(128)}, u32[]{:S(2)}) copy-start(s32[128]{0:T(128)} %param.11) | copy-start | bytes 1540
  1.3 1.0 %copy-start = (bf16[128,2048]{1,0:T(8,128)(2,1)S(1)}, bf16[128,2048]{1,0:T(8,128)(2,1)}, u32[]{:S(2)}) copy-start(bf16[128,2048]{1,0:T(8,128)(2,1)} %q_hbm.1) | copy-start | bytes 1572868
  2.4 0.8 %copy-start.1 = (bf16[128,256]{1,0:T(8,128)(2,1)S(1)}, bf16[128,256]{1,0:T(8,128)(2,1)}, u32[]{:S(2)}) copy-start(bf16[128,256]{1,0:T(8,128)(2,1)} %k_hbm.1) | copy-start | bytes 196612
  3.2 0.8 %copy-start.2 = (bf16[128,256]{1,0:T(8,128)(2,1)S(1)}, bf16[128,256]{1,0:T(8,128)(2,1)}, u32[]{:S(2)}) copy-start(bf16[128,256]{1,0:T(8,128)(2,1)} %v_hbm.1) | copy-start | bytes 196612

commit v2 on v1

--- a/solution.py
+++ b/solution.py
@@ -20,32 +20,45 @@
 NY = 8
 UNIT = 512
 MASKED = -1e30
-SUB_ROWS = ((0, 256), (256, 272))
 ITEM_ROWS = 528
 
 PLAN = {
+    "parts": [
+        (0, 128), (128, 128), (256, 128), (384, 144),
+    ],
     "edges": [
-        (0, (0, 1), (0, 0)), (0, (1, 0), (0, 0)), (0, (-1, 0), (0, 0)), (0, (1, 1), (1, 0)), (0, (-1, 1), (-1, 0)),
-        (0, (2, 0), (1, 0)), (0, (-2, 0), (-1, 0)), (0, (2, 1), (2, 0)), (0, (-2, 1), (-2, 0)), (0, (3, 0), (2, 0)),
-        (0, (-3, 0), (-2, 0)), (0, (3, 1), (3, 0)), (0, (-3, 1), (-3, 0)), (0, (4, 0), (3, 0)), (0, (4, 1), (3, 1)),
-        (1, (0, 1), (0, 0)), (1, (1, 0), (0, 0)), (1, (-1, 0), (0, 0)), (1, (1, 1), (0, 1)), (1, (-1, 1), (0, 1)),
-        (1, (2, 0), (1, 0)), (1, (-2, 0), (-1, 0)), (1, (2, 1), (1, 1)), (1, (-2, 1), (-1, 1)), (1, (3, 0), (2, 0)),
-        (1, (-3, 0), (-2, 0)), (1, (3, 1), (2, 1)), (1, (-3, 1), (-2, 1)), (1, (-4, 0), (-3, 0)),
-        (1, (-4, 1), (-4, 0)),
+        (0, (-3, 0), (-2, 0)), (0, (-3, 1), (-2, 1)), (0, (-2, 0), (-1, 0)), (0, (-2, 1), (-1, 1)),
+        (0, (-1, 0), (0, 0)), (0, (-1, 1), (-1, 0)), (0, (0, 1), (0, 0)), (0, (1, 0), (0, 0)), (0, (1, 1), (0, 1)),
+        (0, (2, 0), (1, 0)), (0, (2, 1), (1, 1)), (0, (3, 0), (2, 0)), (0, (3, 1), (2, 1)), (0, (4, 0), (-3, 0)),
+        (0, (4, 1), (-3, 1)), (1, (-3, 0), (-2, 0)), (1, (-3, 1), (-3, 0)), (1, (-2, 0), (-1, 0)),
+        (1, (-2, 1), (-2, 0)), (1, (-1, 0), (0, 0)), (1, (-1, 1), (-1, 0)), (1, (0, 1), (0, 0)),
+        (1, (1, 0), (0, 0)), (1, (1, 1), (0, 1)), (1, (2, 0), (1, 0)), (1, (2, 1), (1, 1)), (1, (3, 0), (2, 0)),
+        (1, (3, 1), (2, 1)), (1, (4, 0), (-3, 0)), (1, (4, 1), (-3, 1)), (2, (-3, 0), (-2, 0)),
+        (2, (-3, 1), (-3, 0)), (2, (-2, 0), (-1, 0)), (2, (-2, 1), (-2, 0)), (2, (-1, 0), (0, 0)),
+        (2, (-1, 1), (-1, 0)), (2, (0, 1), (0, 0)), (2, (1, 0), (0, 0)), (2, (1, 1), (1, 0)), (2, (2, 0), (1, 0)),
+        (2, (2, 1), (1, 1)), (2, (3, 0), (2, 0)), (2, (3, 1), (2, 1)), (2, (4, 0), (-3, 0)), (2, (4, 1), (4, 0)),
+        (3, (-3, 0), (-2, 0)), (3, (-3, 1), (-2, 1)), (3, (-2, 0), (-1, 0)), (3, (-2, 1), (-2, 0)),
+        (3, (-1, 0), (0, 0)), (3, (-1, 1), (0, 1)), (3, (0, 1), (0, 0)), (3, (1, 0), (0, 0)), (3, (1, 1), (1, 0)),
+        (3, (2, 0), (1, 0)), (3, (2, 1), (2, 0)), (3, (3, 0), (2, 0)), (3, (3, 1), (3, 0)), (3, (4, 0), (-3, 0)),
+        (3, (4, 1), (-3, 1)),
     ],
     "waits": [
-        (0, (0, 1)), (0, (1, 0)), (0, (-1, 0)), (1, (0, 1)), (1, (1, 0)), (1, (-1, 0)), (0, (1, 1)), (0, (2, 0)),
-        (0, (-2, 0)), (0, (-1, 1)), (1, (1, 1)), (1, (-2, 0)), (1, (-1, 1)), (1, (2, 0)), (0, (2, 1)), (0, (-2, 1)),
-        (0, (-3, 0)), (0, (3, 0)), (1, (2, 1)), (1, (-3, 0)), (1, (-2, 1)), (1, (3, 0)), (0, (-3, 1)), (0, (3, 1)),
-        (0, (4, 0)), (1, (-4, 0)), (1, (3, 1)), (1, (-3, 1)), (0, (4, 1)), (1, (-4, 1)),
+        (0, (0, 1)), (0, (-1, 0)), (1, (0, 1)), (1, (-1, 0)), (0, (1, 0)), (2, (0, 1)), (2, (-1, 0)), (3, (0, 1)),
+        (1, (1, 0)), (2, (1, 0)), (3, (-1, 0)), (0, (-1, 1)), (3, (1, 0)), (0, (1, 1)), (1, (-1, 1)), (1, (-2, 0)),
+        (0, (-2, 0)), (2, (-1, 1)), (1, (1, 1)), (2, (-2, 0)), (0, (2, 0)), (2, (1, 1)), (3, (-1, 1)), (3, (-2, 0)),
+        (1, (2, 0)), (3, (1, 1)), (0, (-2, 1)), (2, (2, 0)), (3, (2, 0)), (1, (-3, 0)), (0, (-3, 0)), (1, (-2, 1)),
+        (0, (2, 1)), (3, (-2, 1)), (2, (-2, 1)), (2, (-3, 0)), (3, (-3, 0)), (0, (3, 0)), (1, (2, 1)), (2, (2, 1)),
+        (3, (2, 1)), (1, (4, 0)), (1, (-3, 1)), (1, (3, 0)), (2, (3, 0)), (0, (-3, 1)), (3, (3, 0)), (0, (4, 0)),
+        (3, (-3, 1)), (2, (-3, 1)), (2, (4, 0)), (0, (3, 1)), (3, (4, 0)), (1, (3, 1)), (1, (4, 1)), (2, (3, 1)),
+        (3, (3, 1)), (2, (4, 1)), (3, (4, 1)), (0, (4, 1)),
     ],
     "steps": [
-        [(0, 0)], [(0, 1), (1, 0)], [(-1, 0), (1, 1)], [(-2, 0), (-1, 1)], [(2, 0), (2, 1)], [(-3, 0), (-2, 1)],
-        [(3, 0), (4, 0)], [(3, 1), (-3, 1)], [(4, 1)],
+        [(0, 0)], [(0, 1), (-1, 0)], [(1, 0), (-1, 1)], [(-2, 0), (1, 1)], [(2, 0), (-2, 1)], [(-3, 0), (2, 1)],
+        [(3, 0), (-3, 1)], [(4, 0), (3, 1)], [(4, 1)],
     ],
     "before": [
-        0, 0, 0, 0, 6, 6, 6, 6, 11, 11, 12, 14, 16, 18, 18, 18, 19, 20, 22, 22, 25, 25, 25, 27, 28, 28, 28, 29, 29,
-        29, 30, 30, 30, 30, 30, 30,
+        0, 0, 0, 0, 11, 11, 13, 17, 23, 23, 25, 26, 29, 30, 33, 35, 36, 36, 36, 37, 45, 45, 48, 50, 51, 51, 52, 53,
+        57, 57, 57, 57, 60, 60, 60, 60,
     ],
 }
 
@@ -67,9 +80,20 @@
     return sine_out, cosine_out
 
 
+def frequencies():
+    row = lax.broadcasted_iota(jnp.int32, (8, ROWS), 0)
+    tiles = []
+    for first in range(0, HALF, 8):
+        tile = jnp.zeros((8, ROWS), jnp.float32)
+        for i in range(8):
+            tile = jnp.where(row == i, float(np.float32(ROPE_BASE ** (-2.0 * (first + i) / HEAD_WIDTH))), tile)
+        tiles.append(tile)
+    return jnp.concatenate(tiles, axis=0)
+
+
 def kernel(
-    q_hbm, k_hbm, v_hbm, pos_hbm, reset_hbm, freq_hbm, out_hbm,
-    q_in, k_in, v_in, pos_in, reset_in, freq_in,
+    q_hbm, k_hbm, v_hbm, pos_hbm, reset_hbm, out_ref,
+    q_in, k_in, v_in, pos_in, reset_in,
     items, stage, q_t, q_stage, place, place_sib, bounds, mask, top, total, acc, out_buf,
     in_sem, item_sem, sib_sem, send_sem, out_sem,
 ):
@@ -87,9 +111,12 @@
     sibling = device(y, z, 1 - core)
 
     barrier = pltpu.get_barrier_semaphore()
-    for other in (
-        device(around(y + 1), z, core), device(around(y - 1), z, core), device(y, 1 - z, core), sibling,
-    ):
+    strides = set()
+    for _, node, parent in PLAN["edges"]:
+        stride = ((node[0] - parent[0]) % NY, node[1] ^ parent[1])
+        strides |= {stride, (-stride[0] % NY, stride[1])}
+    partners = [device(around(y + dy), z if dz == 0 else 1 - z, core) for dy, dz in sorted(strides)] + [sibling]
+    for other in partners:
         pl.semaphore_signal(barrier, inc=1, device_id=other, device_id_type=MESH)
 
     def head_cols(slot, width):
@@ -99,21 +126,20 @@
     loads = [
         pltpu.make_async_copy(pos_hbm, pos_in, in_sem.at[0]),
         pltpu.make_async_copy(reset_hbm, reset_in, in_sem.at[1]),
-        pltpu.make_async_copy(freq_hbm, freq_in, in_sem.at[2]),
     ]
     for slot in (1, 0):
-        loads.append(pltpu.make_async_copy(k_hbm.at[:, head_cols(slot, HEAD_WIDTH)], k_in.at[slot], in_sem.at[3 + slot]))
-        loads.append(pltpu.make_async_copy(v_hbm.at[:, head_cols(slot, HEAD_WIDTH)], v_in.at[slot], in_sem.at[5 + slot]))
+        loads.append(pltpu.make_async_copy(k_hbm.at[:, head_cols(slot, HEAD_WIDTH)], k_in.at[slot], in_sem.at[2 + slot]))
+        loads.append(pltpu.make_async_copy(v_hbm.at[:, head_cols(slot, HEAD_WIDTH)], v_in.at[slot], in_sem.at[4 + slot]))
     for slot in (1, 0):
-        loads.append(pltpu.make_async_copy(q_hbm.at[:, head_cols(slot, COLS)], q_in.at[slot], in_sem.at[7 + slot]))
+        loads.append(pltpu.make_async_copy(q_hbm.at[:, head_cols(slot, COLS)], q_in.at[slot], in_sem.at[6 + slot]))
     for load in loads:
         load.start()
 
-    for load in loads[:3]:
+    for load in loads[:2]:
         load.wait()
-    pos = pos_in[...].astype(jnp.float32)
-    reset = reset_in[...].astype(jnp.float32)
-    sine, cosine = sine_cosine(freq_in[...] * reset)
+    pos = pos_in[...].reshape(1, ROWS).astype(jnp.float32)
+    reset = reset_in[...].reshape(1, ROWS).astype(jnp.float32)
+    sine, cosine = sine_cosine(frequencies() * reset)
     sine_rows = jnp.concatenate([-sine, sine], axis=0).T
     cosine_rows = jnp.concatenate([cosine, cosine], axis=0).T
     place[...] = jnp.concatenate([pos, pos - reset, jnp.zeros((6, ROWS), jnp.float32)], axis=0)
@@ -121,7 +147,7 @@
     sine_q, cosine_q = sine * SCALE, cosine * SCALE
 
     my_slot = y * 2 + z
-    for load in loads[3:7]:
+    for load in loads[2:6]:
         load.wait()
 
     def keys_of(slot):
@@ -136,7 +162,7 @@
     items[my_slot, 0:ROWS] = keys_of(0)
     items[my_slot, ROWS : 2 * ROWS] = values_of(0)
 
-    pl.semaphore_wait(barrier, 4)
+    pl.semaphore_wait(barrier, len(partners))
 
     to_sibling = [
         pltpu.make_async_remote_copy(
@@ -154,7 +180,7 @@
     ]
 
     def part_copy(sub, slot, target):
-        rows = items.at[slot, pl.ds(*SUB_ROWS[sub])]
+        rows = items.at[slot, pl.ds(*PLAN["parts"][sub])]
         return pltpu.make_async_remote_copy(
             src_ref=rows, dst_ref=rows, send_sem=send_sem, recv_sem=item_sem.at[sub, slot],
             device_id=target, device_id_type=MESH,
@@ -191,11 +217,11 @@
 
     to_sibling[0].start()
     to_sibling[1].start()
-    hand_on(0, (0, 0))
-
+    for part, (first, _) in enumerate(PLAN["parts"]):
+        if first < 256:
+            hand_on(part, (0, 0))
     loads[7].wait()
-    rotate_queries(1)
-    to_sibling[2].start()
+    rotate_queries(0)
 
     to_sibling[0].wait_recv()
     bounds[1] = place_sib[...]
@@ -208,10 +234,13 @@
         place_rows + [jnp.zeros((12, ROWS), jnp.float32)], axis=0
     ).astype(jnp.bfloat16)
     to_sibling[1].wait_recv()
-    hand_on(1, (0, 0))
-
-    loads[8].wait()
-    rotate_queries(0)
+    for part, (first, _) in enumerate(PLAN["parts"]):
+        if first >= 256:
+            hand_on(part, (0, 0))
+
+    loads[6].wait()
+    rotate_queries(1)
+    to_sibling[2].start()
     unit_matrix = (
         lax.broadcasted_iota(jnp.int32, (ROWS, ROWS), 0) == lax.broadcasted_iota(jnp.int32, (ROWS, ROWS), 1)
     ).astype(jnp.float32).astype(jnp.bfloat16)
@@ -220,10 +249,11 @@
     top[...] = jnp.full_like(top, MASKED)
     total[...] = jnp.zeros_like(total)
     acc[...] = jnp.zeros_like(acc)
-    to_sibling[2].wait_recv()
 
     steps = PLAN["steps"]
-    units = [(step, unit) for step in range(len(steps)) for unit in range(2 * COLS // UNIT)]
+    per_step = 2 * COLS // UNIT
+    units = [(0, unit) for unit in range(per_step)]
+    units += [(step, unit) for step in range(1, len(steps)) for unit in reversed(range(per_step))]
 
     def prepare(step):
         row = 0
@@ -270,15 +300,16 @@
     def finish(group):
         for head in range(GROUP):
             cols = slice(group * COLS + head * ROWS, group * COLS + (head + 1) * ROWS)
-            result = acc[:, cols] / total[:, cols]
-            out_buf[group, :, head * ROWS : (head + 1) * ROWS] = result.T.astype(jnp.bfloat16)
-
-    out_cols = pl.ds(pl.multiple_of(core * COLS, COLS), COLS)
+            result = (acc[:, cols] / total[:, cols]).T.astype(jnp.bfloat16)
+            if group == 0:
+                out_ref[:, pl.ds(pl.multiple_of(core * COLS + head * ROWS, ROWS), ROWS)] = result
+            else:
+                out_buf[:, head * ROWS : (head + 1) * ROWS] = result
+
     back = pltpu.make_async_remote_copy(
-        src_ref=out_buf.at[1], dst_ref=out_hbm.at[:, out_cols], send_sem=out_sem.at[0], recv_sem=out_sem.at[1],
-        device_id=sibling, device_id_type=MESH,
+        src_ref=out_buf, dst_ref=out_ref.at[:, pl.ds(pl.multiple_of(core * COLS, COLS), COLS)],
+        send_sem=out_sem.at[0], recv_sem=out_sem.at[1], device_id=sibling, device_id_type=MESH,
     )
-    keep = pltpu.make_async_copy(out_buf.at[0], out_hbm.at[:, out_cols], out_sem.at[2])
 
     waits = PLAN["waits"]
     made = 0
@@ -292,11 +323,12 @@
     def scores_of(index):
         make_waits(PLAN["before"][index])
         step, unit = units[index]
-        if unit == UNIT_ORDER[0]:
+        if index % per_step == 0:
             prepare(step)
+        if index == per_step // 2:
+            to_sibling[2].wait_recv()
         return score(step, unit)
 
-    units = [(step, unit) for step in range(len(steps)) for unit in UNIT_ORDER]
     coming = scores_of(0)
     pending = None
     for index, (step, unit) in enumerate(units):
@@ -307,42 +339,33 @@
         if pending is not None:
             gather_values(*pending)
         pending = (step, unit, weights, rescale)
-        if index == len(units) - 2:
-            pass
+        if index == len(units) - per_step // 2:
+            finish(1)
+            back.start()
     gather_values(*pending)
-    finish(1)
-    back.start()
     finish(0)
-    keep.start()
 
     all_parts = items.at[pl.ds(0, 2 * NY - 1)]
     pltpu.make_async_copy(all_parts, all_parts, send_sem).wait()
     for copy in to_sibling:
         copy.wait_send()
     back.wait()
-    keep.wait()
-
-
-UNIT_ORDER = tuple(range(2 * COLS // UNIT))[::-1]
 
 
 def on_device(queries, keys, values, loader_pos, reset_pos, doc_starts):
     del doc_starts
-    frequency = (ROPE_BASE ** (-np.arange(HALF, dtype=np.float64) * 2.0 / HEAD_WIDTH)).astype(np.float32)
-    frequency = jnp.asarray(np.broadcast_to(frequency[:, None], (HALF, ROWS)))
     bf16, f32 = jnp.bfloat16, jnp.float32
     return pl.pallas_call(
         kernel,
-        out_shape=jax.ShapeDtypeStruct((ROWS, 2 * COLS), bf16),
-        in_specs=[pl.BlockSpec(memory_space=pl.ANY)] * 6,
-        out_specs=pl.BlockSpec(memory_space=pl.ANY),
+        out_shape=pltpu.VMEM((ROWS, 2 * COLS), bf16),
+        in_specs=[pl.BlockSpec(memory_space=pltpu.HBM)] * 5,
+        out_specs=pl.BlockSpec(memory_space=pltpu.VMEM),
         scratch_shapes=[
             pltpu.VMEM((2, ROWS, COLS), bf16),
             pltpu.VMEM((2, ROWS, HEAD_WIDTH), bf16),
             pltpu.VMEM((2, ROWS, HEAD_WIDTH), bf16),
-            pltpu.VMEM((1, ROWS), jnp.int32),
-            pltpu.VMEM((1, ROWS), jnp.int32),
-            pltpu.VMEM((HALF, ROWS), f32),
+            pltpu.VMEM((ROWS,), jnp.int32),
+            pltpu.VMEM((ROWS,), jnp.int32),
             pltpu.VMEM((2 * NY, ITEM_ROWS, HEAD_WIDTH), bf16),
             pltpu.VMEM((256, HEAD_WIDTH), bf16),
             pltpu.VMEM((2 * HEAD_WIDTH, 2 * COLS), bf16),
@@ -354,17 +377,17 @@
             pltpu.VMEM((1, 2 * COLS), f32),
             pltpu.VMEM((1, 2 * COLS), f32),
             pltpu.VMEM((HEAD_WIDTH, 2 * COLS), f32),
-            pltpu.VMEM((2, ROWS, COLS), bf16),
-            pltpu.SemaphoreType.DMA((9,)),
-            pltpu.SemaphoreType.DMA((2, 2 * NY)),
+            pltpu.VMEM((ROWS, COLS), bf16),
+            pltpu.SemaphoreType.DMA((8,)),
+            pltpu.SemaphoreType.DMA((len(PLAN["parts"]), 2 * NY)),
             pltpu.SemaphoreType.DMA((6,)),
             pltpu.SemaphoreType.DMA,
-            pltpu.SemaphoreType.DMA((3,)),
+            pltpu.SemaphoreType.DMA((2,)),
         ],
         compiler_params=pltpu.CompilerParams(
-            collective_id=0, has_side_effects=True, vmem_limit_bytes=48 * 2**20
+            collective_id=0, has_side_effects=True, vmem_limit_bytes=60 * 2**20
         ),
-    )(queries, keys, values, loader_pos.reshape(1, ROWS), reset_pos.reshape(1, ROWS), frequency)
+    )(*(pltpu.with_memory_space_constraint(x, pltpu.HBM) for x in (queries, keys, values, loader_pos, reset_pos)))
 
 
 def solution(mesh):

time: 39.2 us -> 33 us (0.84)
  local copies, waits for them, and re-layouts: 4.84 us -> 0.8 us
  Pallas kernels: 34 us -> 32.1 us
    unnamed x13 -> x1, local copies, waits for them, and re-layouts: 4.77 us -> 0.8 us
    pallas_call x1, Pallas kernels: 34 us -> 32.1 us  [on_device(): pl.pallas_call(kernel, out_shape=pltpu.VMEM((ROWS, 2 * COLS), bf16), in_s...]
where the time goes in v2:
time: 33 us; the launch traced here: 32.9 us
  Pallas kernels  32.1 us (97%)
  local copies, waits for them, and re-layouts  0.8 us (2%)
    pallas_call x1, Pallas kernels, on_device(): pl.pallas_call(kernel, out_shape=pltpu.VMEM((ROWS, 2 * COLS), bf16), in_s...  32.1 us
    unnamed x1, local copies, waits for them, and re-layouts  0.8 us

profile of v2, /device:TPU:1, one launch (start us, length us, event | category | flops | bytes accessed | tf_op | source)
XLA Modules:
  0.0 32.9 jit_solution(8857964174915985821)
XLA Ops:
  0.0 32.1 %shard_map.55 = bf16[128,2048]{1,0:T(8,128)(2,1)S(1)} custom-call(bf16[128,2048]{1,0:T(8,128)(2,1)} %q_hbm.1, bf16[128,256]{1,0:T(8,128)(2,1)} %k_hbm.1, bf16[128,256]{1,0:T(8,128)(2,1)} %v_hbm.1, s32[128]{0:T(128)} %pos_hbm.1, s32[128]{0:T(128)} %reset_hbm.1), custom_call_target="tpu_custom_call" | custom-call | tf_op jit(solution)/shard_map/pallas_call | solution.py:358
  32.1 0.8 %copy.7 = bf16[128,2048]{1,0:T(8,128)(2,1)} copy(bf16[128,2048]{1,0:T(8,128)(2,1)S(1)} %shard_map.55) | data formatting | bytes 1048576

commit v3 on v2

--- a/solution.py
+++ b/solution.py
@@ -24,41 +24,30 @@
 
 PLAN = {
     "parts": [
-        (0, 128), (128, 128), (256, 128), (384, 144),
+        (0, 256), (256, 272),
     ],
     "edges": [
-        (0, (-3, 0), (-2, 0)), (0, (-3, 1), (-2, 1)), (0, (-2, 0), (-1, 0)), (0, (-2, 1), (-1, 1)),
-        (0, (-1, 0), (0, 0)), (0, (-1, 1), (-1, 0)), (0, (0, 1), (0, 0)), (0, (1, 0), (0, 0)), (0, (1, 1), (0, 1)),
-        (0, (2, 0), (1, 0)), (0, (2, 1), (1, 1)), (0, (3, 0), (2, 0)), (0, (3, 1), (2, 1)), (0, (4, 0), (-3, 0)),
+        (0, (-3, 0), (-2, 0)), (0, (-3, 1), (-3, 0)), (0, (-2, 0), (-1, 0)), (0, (-2, 1), (-2, 0)),
+        (0, (-1, 0), (0, 0)), (0, (-1, 1), (-1, 0)), (0, (0, 1), (0, 0)), (0, (1, 0), (0, 0)), (0, (1, 1), (1, 0)),
+        (0, (2, 0), (1, 0)), (0, (2, 1), (1, 1)), (0, (3, 0), (2, 0)), (0, (3, 1), (3, 0)), (0, (4, 0), (-3, 0)),
         (0, (4, 1), (-3, 1)), (1, (-3, 0), (-2, 0)), (1, (-3, 1), (-3, 0)), (1, (-2, 0), (-1, 0)),
-        (1, (-2, 1), (-2, 0)), (1, (-1, 0), (0, 0)), (1, (-1, 1), (-1, 0)), (1, (0, 1), (0, 0)),
-        (1, (1, 0), (0, 0)), (1, (1, 1), (0, 1)), (1, (2, 0), (1, 0)), (1, (2, 1), (1, 1)), (1, (3, 0), (2, 0)),
-        (1, (3, 1), (2, 1)), (1, (4, 0), (-3, 0)), (1, (4, 1), (-3, 1)), (2, (-3, 0), (-2, 0)),
-        (2, (-3, 1), (-3, 0)), (2, (-2, 0), (-1, 0)), (2, (-2, 1), (-2, 0)), (2, (-1, 0), (0, 0)),
-        (2, (-1, 1), (-1, 0)), (2, (0, 1), (0, 0)), (2, (1, 0), (0, 0)), (2, (1, 1), (1, 0)), (2, (2, 0), (1, 0)),
-        (2, (2, 1), (1, 1)), (2, (3, 0), (2, 0)), (2, (3, 1), (2, 1)), (2, (4, 0), (-3, 0)), (2, (4, 1), (4, 0)),
-        (3, (-3, 0), (-2, 0)), (3, (-3, 1), (-2, 1)), (3, (-2, 0), (-1, 0)), (3, (-2, 1), (-2, 0)),
-        (3, (-1, 0), (0, 0)), (3, (-1, 1), (0, 1)), (3, (0, 1), (0, 0)), (3, (1, 0), (0, 0)), (3, (1, 1), (1, 0)),
-        (3, (2, 0), (1, 0)), (3, (2, 1), (2, 0)), (3, (3, 0), (2, 0)), (3, (3, 1), (3, 0)), (3, (4, 0), (-3, 0)),
-        (3, (4, 1), (-3, 1)),
+        (1, (-2, 1), (-1, 1)), (1, (-1, 0), (0, 0)), (1, (-1, 1), (-1, 0)), (1, (0, 1), (0, 0)),
+        (1, (1, 0), (0, 0)), (1, (1, 1), (0, 1)), (1, (2, 0), (1, 0)), (1, (2, 1), (2, 0)), (1, (3, 0), (2, 0)),
+        (1, (3, 1), (2, 1)), (1, (4, 0), (-3, 0)), (1, (4, 1), (4, 0)),
     ],
     "waits": [
-        (0, (0, 1)), (0, (-1, 0)), (1, (0, 1)), (1, (-1, 0)), (0, (1, 0)), (2, (0, 1)), (2, (-1, 0)), (3, (0, 1)),
-        (1, (1, 0)), (2, (1, 0)), (3, (-1, 0)), (0, (-1, 1)), (3, (1, 0)), (0, (1, 1)), (1, (-1, 1)), (1, (-2, 0)),
-        (0, (-2, 0)), (2, (-1, 1)), (1, (1, 1)), (2, (-2, 0)), (0, (2, 0)), (2, (1, 1)), (3, (-1, 1)), (3, (-2, 0)),
-        (1, (2, 0)), (3, (1, 1)), (0, (-2, 1)), (2, (2, 0)), (3, (2, 0)), (1, (-3, 0)), (0, (-3, 0)), (1, (-2, 1)),
-        (0, (2, 1)), (3, (-2, 1)), (2, (-2, 1)), (2, (-3, 0)), (3, (-3, 0)), (0, (3, 0)), (1, (2, 1)), (2, (2, 1)),
-        (3, (2, 1)), (1, (4, 0)), (1, (-3, 1)), (1, (3, 0)), (2, (3, 0)), (0, (-3, 1)), (3, (3, 0)), (0, (4, 0)),
-        (3, (-3, 1)), (2, (-3, 1)), (2, (4, 0)), (0, (3, 1)), (3, (4, 0)), (1, (3, 1)), (1, (4, 1)), (2, (3, 1)),
-        (3, (3, 1)), (2, (4, 1)), (3, (4, 1)), (0, (4, 1)),
+        (0, (-1, 0)), (0, (1, 0)), (0, (0, 1)), (1, (-1, 0)), (1, (1, 0)), (1, (0, 1)), (0, (-2, 0)), (0, (-1, 1)),
+        (1, (-2, 0)), (0, (1, 1)), (0, (2, 0)), (1, (-1, 1)), (1, (2, 0)), (0, (-3, 0)), (1, (-3, 0)), (1, (1, 1)),
+        (0, (-2, 1)), (1, (2, 1)), (0, (2, 1)), (0, (3, 0)), (1, (-2, 1)), (0, (-3, 1)), (0, (4, 0)), (1, (4, 0)),
+        (1, (-3, 1)), (1, (3, 0)), (1, (3, 1)), (0, (3, 1)), (0, (4, 1)), (1, (4, 1)),
     ],
     "steps": [
-        [(0, 0)], [(0, 1), (-1, 0)], [(1, 0), (-1, 1)], [(-2, 0), (1, 1)], [(2, 0), (-2, 1)], [(-3, 0), (2, 1)],
-        [(3, 0), (-3, 1)], [(4, 0), (3, 1)], [(4, 1)],
+        [(0, 0)], [(-1, 0), (1, 0)], [(0, 1), (-2, 0)], [(-1, 1), (2, 0)], [(-3, 0), (1, 1)], [(2, 1), (-2, 1)],
+        [(4, 0), (-3, 1)], [(3, 0), (3, 1)], [(4, 1)],
     ],
     "before": [
-        0, 0, 0, 0, 11, 11, 13, 17, 23, 23, 25, 26, 29, 30, 33, 35, 36, 36, 36, 37, 45, 45, 48, 50, 51, 51, 52, 53,
-        57, 57, 57, 57, 60, 60, 60, 60,
+        0, 0, 0, 0, 5, 7, 7, 7, 10, 10, 14, 14, 14, 14, 15, 17, 17, 17, 18, 19, 22, 22, 22, 25, 26, 26, 26, 26, 28,
+        28, 28, 28, 30, 30, 30, 30,
     ],
 }
 

time: 33 us -> 32.6 us (0.988)
  Pallas kernels: 32.1 us -> 31.6 us
    pallas_call x1, Pallas kernels: 32.1 us -> 31.6 us  [on_device(): pl.pallas_call(kernel, out_shape=pltpu.VMEM((ROWS, 2 * COLS), bf16), in_s...]
where the time goes in v3:
time: 32.6 us; the launch traced here: 32.5 us
  Pallas kernels  31.6 us (97%)
  local copies, waits for them, and re-layouts  0.8 us (2%)
    pallas_call x1, Pallas kernels, on_device(): pl.pallas_call(kernel, out_shape=pltpu.VMEM((ROWS, 2 * COLS), bf16), in_s...  31.6 us
    unnamed x1, local copies, waits for them, and re-layouts  0.8 us

profile of v3, /device:TPU:1, one launch (start us, length us, event | category | flops | bytes accessed | tf_op | source)
XLA Modules:
  0.0 32.5 jit_solution(5751885440644496510)
XLA Ops:
  0.0 31.6 %shard_map.55 = bf16[128,2048]{1,0:T(8,128)(2,1)S(1)} custom-call(bf16[128,2048]{1,0:T(8,128)(2,1)} %q_hbm.1, bf16[128,256]{1,0:T(8,128)(2,1)} %k_hbm.1, bf16[128,256]{1,0:T(8,128)(2,1)} %v_hbm.1, s32[128]{0:T(128)} %pos_hbm.1, s32[128]{0:T(128)} %reset_hbm.1), custom_call_target="tpu_custom_call" | custom-call | tf_op jit(solution)/shard_map/pallas_call | solution.py:347
  31.7 0.8 %copy.7 = bf16[128,2048]{1,0:T(8,128)(2,1)} copy(bf16[128,2048]{1,0:T(8,128)(2,1)S(1)} %shard_map.55) | data formatting | bytes 1048576

commit v4 on v3

--- a/solution.py
+++ b/solution.py
@@ -151,6 +151,15 @@
     items[my_slot, 0:ROWS] = keys_of(0)
     items[my_slot, ROWS : 2 * ROWS] = values_of(0)
 
+    unit_matrix = (
+        lax.broadcasted_iota(jnp.int32, (ROWS, ROWS), 0) == lax.broadcasted_iota(jnp.int32, (ROWS, ROWS), 1)
+    ).astype(jnp.float32).astype(jnp.bfloat16)
+    for head in range(2 * GROUP):
+        q_t[HEAD_WIDTH:, head * ROWS : (head + 1) * ROWS] = unit_matrix
+    top[...] = jnp.full_like(top, MASKED)
+    total[...] = jnp.zeros_like(total)
+    acc[...] = jnp.zeros_like(acc)
+
     pl.semaphore_wait(barrier, len(partners))
 
     to_sibling = [
@@ -230,15 +239,6 @@
     loads[6].wait()
     rotate_queries(1)
     to_sibling[2].start()
-    unit_matrix = (
-        lax.broadcasted_iota(jnp.int32, (ROWS, ROWS), 0) == lax.broadcasted_iota(jnp.int32, (ROWS, ROWS), 1)
-    ).astype(jnp.float32).astype(jnp.bfloat16)
-    for head in range(2 * GROUP):
-        q_t[HEAD_WIDTH:, head * ROWS : (head + 1) * ROWS] = unit_matrix
-    top[...] = jnp.full_like(top, MASKED)
-    total[...] = jnp.zeros_like(total)
-    acc[...] = jnp.zeros_like(acc)
-
     steps = PLAN["steps"]
     per_step = 2 * COLS // UNIT
     units = [(0, unit) for unit in range(per_step)]

time: 32.6 us -> 32.6 us (level)
  no operation moved by 1% of the time
where the time goes in v4:
time: 32.6 us; the launch traced here: 32.4 us
  Pallas kernels  31.6 us (97%)
  local copies, waits for them, and re-layouts  0.8 us (2%)
    pallas_call x1, Pallas kernels, on_device(): pl.pallas_call(kernel, out_shape=pltpu.VMEM((ROWS, 2 * COLS), bf16), in_s...  31.6 us
    unnamed x1, local copies, waits for them, and re-layouts  0.8 us

profile of v4, /device:TPU:1, one launch (start us, length us, event | category | flops | bytes accessed | tf_op | source)
XLA Modules:
  0.0 32.4 jit_solution(9675733453946183587)
XLA Ops:
  0.0 31.6 %shard_map.55 = bf16[128,2048]{1,0:T(8,128)(2,1)S(1)} custom-call(bf16[128,2048]{1,0:T(8,128)(2,1)} %q_hbm.1, bf16[128,256]{1,0:T(8,128)(2,1)} %k_hbm.1, bf16[128,256]{1,0:T(8,128)(2,1)} %v_hbm.1, s32[128]{0:T(128)} %pos_hbm.1, s32[128]{0:T(128)} %reset_hbm.1), custom_call_target="tpu_custom_call" | custom-call | tf_op jit(solution)/shard_map/pallas_call | solution.py:347
  31.6 0.8 %copy.7 = bf16[128,2048]{1,0:T(8,128)(2,1)} copy(bf16[128,2048]{1,0:T(8,128)(2,1)S(1)} %shard_map.55) | data formatting | bytes 1048576
